TPU v7x, 32 devices: a whole 2x2x4 slice. The times are simulated.
32 devices in a mesh: group: 2 (over x), adapter: 16 (over z, y, core).
Axes of the slice: x: 2, y: 2, z: 4, core: 2. Of those that a mesh axis runs over, the one named last changes fastest.
Arguments:
- tokens: bfloat16 [1024, 8192], P(('group', 'adapter')), parts along dimension 0, may hold values from -6 to 6
- kept_weight_entries: bfloat16 [4096, 28672], P(None, 'adapter'), may hold values from -0.09375 to 0.09375
- kept_row_pattern: int32 [2048, 28672], P(None, 'adapter'), may hold values from 0 to 5
- request_adapter: int32 [1024, 1], P('group'), parts along dimension 0, may hold values from 0 to 15; in each aligned block of 32 rows (0 to 31, 32 to 63, ...) at most 4 rows name the same one
- adapter_storage_slot: int32 [16], replicated, may hold values from 0 to 15, each once
- adapter_down_maps: bfloat16 [16, 8192, 64], P('adapter'), may hold values from -0.0625 to 0.0625
- adapter_up_maps: bfloat16 [16, 64, 28672], P(None, None, 'adapter'), may hold values from -0.75 to 0.75
Outputs:
- projected: bfloat16 [1024, 28672], P('group', 'adapter'), parts along dimension 0
There are 2 independent parts, one for each index of `group`. A program takes and returns all parts, laid end to end along the dimension named above; an argument that names none is the same for every part. Nothing has to cross between parts.
Inputs may be any that keep to these rules, and one draw needn't show every extreme that they name: `request_adapter`: in each aligned block of 32 requests no adapter is named by more than 4 requests, a bound that some block reaches. `adapter_storage_slot`: each slot holds one adapter.
All inputs are finite; a program needn't handle non-finite values.
Results may differ from a plain program's by a relative error of at most 0.0046.
Values may be sent and summed in bfloat16 or wider, within the bound.
A program may use at most 320 MiB of HBM per device.

v0:
```python
import jax
import jax.numpy as jnp
from jax import lax
from jax.sharding import PartitionSpec as P

ADAPTER_SCALE = 2.0


def expand_sparse(values, pattern):
    quarter = pattern.shape[0]
    width = pattern.shape[1]
    first = (pattern >= 3).astype(jnp.int32) + (pattern >= 5).astype(jnp.int32)
    second = (
        1
        + (pattern == 1).astype(jnp.int32)
        + 2 * (pattern == 2).astype(jnp.int32)
        + (pattern == 3).astype(jnp.int32)
        + 2 * (pattern == 4).astype(jnp.int32)
        + 2 * (pattern == 5).astype(jnp.int32)
    )
    pairs = values.reshape(quarter, 2, width)
    value_one = pairs[:, 0, :]
    value_two = pairs[:, 1, :]
    zeros_row = jnp.zeros_like(value_one)
    placed = [
        jnp.where(first == place, value_one, zeros_row)
        + jnp.where(second == place, value_two, zeros_row)
        for place in range(4)
    ]
    return jnp.stack(placed, axis=1).reshape(quarter * 4, width)


def body(
    tokens,
    kept_weight_entries,
    kept_row_pattern,
    request_adapter,
    adapter_storage_slot,
    adapter_down_maps,
    adapter_up_maps,
):
    holders = lax.axis_size("adapter")
    own_index = lax.axis_index("adapter")
    rows_dev = tokens.shape[0]
    rows_all = rows_dev * holders
    capacity = max(2, 2 * rows_dev // holders)
    adapters = adapter_storage_slot.shape[0]
    low_rank_width = adapter_down_maps.shape[2]
    width = tokens.shape[1]
    dense = expand_sparse(kept_weight_entries, kept_row_pattern)
    local_down_maps = adapter_down_maps[0]
    table = (request_adapter == jnp.arange(adapters, dtype=jnp.int32)[None, :]).astype(jnp.int32)
    row_slot = jnp.sum(table * adapter_storage_slot[None, :], axis=1)
    blocked = row_slot.reshape(holders, rows_dev)
    earlier = (
        jnp.arange(rows_dev, dtype=jnp.int32)[None, :]
        < jnp.arange(rows_dev, dtype=jnp.int32)[:, None]
    )
    same_slot = blocked[:, :, None] == blocked[:, None, :]
    position = jnp.sum((same_slot & earlier[None, :, :]).astype(jnp.int32), axis=2)
    target = blocked * capacity + position
    placing = (
        target[:, :, None] == jnp.arange(holders * capacity, dtype=jnp.int32)[None, None, :]
    ).astype(jnp.bfloat16)
    own_placing = lax.dynamic_index_in_dim(placing, own_index, 0, keepdims=False)
    sparse_output = jnp.dot(
        lax.all_gather(tokens, "adapter", axis=0, tiled=True),
        dense,
        preferred_element_type=jnp.float32,
    )
    outgoing = jnp.dot(own_placing.T, tokens, preferred_element_type=jnp.float32).astype(
        jnp.bfloat16
    )
    outgoing = outgoing.reshape(holders, capacity, width)
    low_buffer = jnp.einsum(
        "skd,dr->skr",
        lax.all_to_all(outgoing, "adapter", split_axis=0, concat_axis=0, tiled=True),
        local_down_maps,
        preferred_element_type=jnp.float32,
    ).astype(jnp.bfloat16)
    returned = lax.all_to_all(
        low_buffer.reshape(holders, capacity * low_rank_width),
        "adapter",
        split_axis=0,
        concat_axis=0,
        tiled=True,
    )
    own_low = jnp.dot(
        own_placing,
        returned.reshape(holders * capacity, low_rank_width),
        preferred_element_type=jnp.float32,
    ).astype(jnp.bfloat16)
    low_rows = lax.all_gather(own_low, "adapter", axis=0, tiled=True)
    slot_onehot = (row_slot[:, None] == jnp.arange(adapters, dtype=jnp.int32)[None, :]).astype(
        jnp.bfloat16
    )
    spread_rows = (slot_onehot[:, :, None] * low_rows[:, None, :]).reshape(
        rows_all, adapters * low_rank_width
    )
    local_hidden = adapter_up_maps.shape[2]
    low_rank_update = jnp.dot(
        spread_rows,
        adapter_up_maps.reshape(adapters * low_rank_width, local_hidden),
        preferred_element_type=jnp.float32,
    )
    return (sparse_output + ADAPTER_SCALE * low_rank_update).astype(jnp.bfloat16)


def solution(mesh):
    placed = (
        P(("group", "adapter"), None),
        P(None, "adapter"),
        P(None, "adapter"),
        P("group", None),
        P(),
        P("adapter", None, None),
        P(None, None, "adapter"),
    )
    return jax.shard_map(
        body, mesh=mesh, in_specs=placed, out_specs=P("group", "adapter"), check_vma=False
    )
```

profile of v0, /device:TPU:1, one launch (start us, length us, event | category | flops | bytes accessed | tf_op | source)
XLA Modules:
  0.0 301.1 jit_solution(6015777692017459990)
XLA Ops:
  6.5 0.0 copy-start
  6.5 0.0 all-gather.2.cloned.1.call-start
  6.5 0.7 all-gather.2.cloned.1.call-update
  7.3 0.8 select_reduce_fusion
  8.1 0.1 reshape.70
  8.1 0.5 convert_reduce_fusion
  8.6 1.6 convolution_convert_fusion
  10.2 1.2 reshape.71
  11.4 7.4 %all-to-all-start = ((bf16[16,4,8192]{2,1,0:T(4,128)(2,1)}), bf16[16,4,8192]{2,1,0:T(4,128)(2,1)}, u32[]{:S(2)}, u32[]{:S(2)}) async-start(bf16[16,4,8192]{2,1,0:T(4,128)(2,1)} %reshape.71), calls=%async_computation | async-start | bytes 2097152 | tf_op jit(solution)/shard_map/all_to_all | solution.py:77
  18.8 29.0 %reshape.68 = bf16[2048,2,1792]{2,1,0:T(2,128)(2,1)} reshape(bf16[4096,1792]{1,0:T(8,128)(2,1)} %param.8) | data formatting | bytes 29360128 | tf_op jit(solution)/shard_map/reshape | solution.py:21
  47.8 28.5 %fusion.29 = (bf16[2048,1,1792]{2,1,0:T(2,128)(2,1)}, bf16[2048,1,1792]{2,1,0:T(2,128)(2,1)}) fusion(bf16[2048,2,1792]{2,1,0:T(2,128)(2,1)} %reshape.68), kind=kLoop, calls=%fused_computation.48 | loop fusion | bytes 29360128 | tf_op jit(solution)/shard_map/slice | solution.py:23
  76.3 0.0 slice-start
  76.3 0.0 slice-start.1
  76.3 0.0 slice-start.2
  76.3 0.0 slice-start.3
  76.3 32.0 %fusion.9 = (bf16[2048,1,1792]{2,0,1:T(8,128)(2,1)}, bf16[2048,1,1792]{2,0,1:T(8,128)(2,1)}, bf16[2048,1,1792]{2,0,1:T(8,128)(2,1)}, pred[2048,1792]{1,0:T(8,128)(4,1)}, pred[2048,1792]{1,0:T(8,128)(4,1)}) fusion(s32[2048,1792]{1,0:T(8,128)} %param.9, bf16[2048,1,1792]{2,1,0:T(2,128)(2,1)} %get-tuple-element.14, bf16[2048,1,1792]{2,1,0:T(2,128)(2,1)} %get-tuple-element.13), kind=kLoop, calls=%fused_computation.17 | loop fusion | flops 91750400 | bytes 58720256 | tf_op jit(solution)/shard_map/stack | solution.py:30
  108.4 0.0 slice-done
  108.4 0.0 slice-done.1
  108.4 0.0 slice-done.2
  108.4 0.0 slice-done.3
  108.4 23.0 %fusion.11 = (bf16[2048,1,1792]{2,0,1:T(8,128)(2,1)}, bf16[2048,1,1792]{2,0,1:T(8,128)(2,1)}, bf16[2048,1,1792]{2,0,1:T(8,128)(2,1)}) fusion(pred[2048,1792]{1,0:T(8,128)(4,1)} %get-tuple-element.9, pred[2048,1792]{1,0:T(8,128)(4,1)} %get-tuple-element.8, bf16[2048,1,1792]{2,0,1:T(8,128)(2,1)} %get-tuple-element.7, ...), kind=kLoop, calls=%fused_computation.19 | loop fusion | flops 121110528 | bytes 58720256 | tf_op jit(solution)/shard_map/stack | solution.py:30
  131.4 20.6 %pad_maximum_fusion = bf16[2048,4,1792]{2,0,1:T(8,128)(2,1)} fusion(bf16[2048,1,1792]{2,0,1:T(8,128)(2,1)} %get-tuple-element.12, bf16[2048,1,1792]{2,0,1:T(8,128)(2,1)} %get-tuple-element.11, bf16[2048,1,1792]{2,0,1:T(8,128)(2,1)} %get-tuple-element.10, bf16[2048,1,1792]{2,0,1:T(8,128)(2,1)} %get-tuple-element.5), kind=kLoop, calls=%fused_computation | loop fusion | flops 44040192 | bytes 58720256 | tf_op jit(solution)/shard_map/stack | solution.py:30
  152.0 0.0 all-to-all-done
  152.0 0.0 copy-done
  152.0 2.0 convolution_convert_fusion.1
  154.0 0.1 all_to_all.12
  154.1 0.5 broadcast.107
  154.7 0.7 reduce.1
  155.3 0.6 reshape.76
  156.0 5.8 %all-to-all-start.1 = ((bf16[16,2,128]{2,1,0:T(2,128)(2,1)}), bf16[16,2,128]{2,1,0:T(2,128)(2,1)S(1)}, u32[]{:S(2)}, u32[]{:S(2)}) async-start(bf16[16,2,128]{2,1,0:T(2,128)(2,1)} %reshape.76), calls=%async_computation.1 | async-start | bytes 16384 | tf_op jit(solution)/shard_map/all_to_all | solution.py:81
  161.7 37.4 %copy.36 = bf16[2048,4,1792]{2,1,0:T(4,128)(2,1)} copy(bf16[2048,4,1792]{2,0,1:T(8,128)(2,1)} %pad_maximum_fusion) | data formatting | bytes 58720256 | tf_op jit(solution)/shard_map/stack | solution.py:30
  199.1 45.2 %reshape.69 = bf16[8192,1792]{1,0:T(8,128)(2,1)} reshape(bf16[2048,4,1792]{2,1,0:T(4,128)(2,1)} %copy.36) | data formatting | bytes 58720256 | tf_op jit(solution)/shard_map/reshape | solution.py:30
  244.3 0.0 all-to-all-done.1
  244.3 0.1 reduce
  244.4 0.1 reshape.72
  244.4 0.2 convolution_convert_fusion.2
  244.6 22.0 %all_gather.7 = bf16[512,64]{1,0:T(8,128)(2,1)S(1)} all-gather(bf16[32,64]{1,0:T(8,128)(2,1)S(1)} %convolution_convert_fusion.2), channel_id=1, replica_groups=mesh['group'=2,'adapter'=16] {'adapter'}, dimensions={0}, use_global_device_ids=true | all-gather | bytes 69632 | tf_op jit(solution)/shard_map/all_gather | solution.py:93
  266.6 0.1 copy.40
  266.7 0.0 all-gather.2.cloned.1.call-done
  266.8 0.0 copy-start.2
  266.8 0.0 copy-start.1
  266.8 22.7 %fusion.30 = f32[1792,512]{1,0:T(8,128)S(1)} fusion(bf16[8192,1792]{1,0:T(8,128)(2,1)} %reshape.69, bf16[512,8192]{1,0:T(8,128)(2,1)} %all-gather.2.cloned.1.call-done), kind=kOutput, calls=%fused_computation.49 | convolution fusion | flops 15032385536 | bytes 41418752 | tf_op jit(solution)/shard_map/dot_general | solution.py:66
  289.4 0.0 copy-done.2
  289.4 2.4 fusion.17
  291.8 2.4 copy.42
  294.2 0.0 copy-done.1
  (7 shorter events, 0.1 us)
Async XLA Ops:
  6.5 145.5 %copy-start = (bf16[1,8192,64]{1,2,0:T(8,128)(2,1)S(1)}, bf16[1,8192,64]{1,2,0:T(8,128)(2,1)}, u32[]{:S(2)}) copy-start(bf16[1,8192,64]{1,2,0:T(8,128)(2,1)} %param.12) | copy-start | bytes 3145732
  6.5 260.2 %all-gather.2.cloned.1.call-start = ((), (), s32[]{:S(2)}) async-start(), calls=%async_computation.2 | async-start | bytes 8912896 | tf_op jit(solution)/shard_map/all_gather | solution.py:67
  11.4 140.5 %all-to-all-start = ((bf16[16,4,8192]{2,1,0:T(4,128)(2,1)}), bf16[16,4,8192]{2,1,0:T(4,128)(2,1)}, u32[]{:S(2)}, u32[]{:S(2)}) async-start(bf16[16,4,8192]{2,1,0:T(4,128)(2,1)} %reshape.71), calls=%async_computation | async-start | bytes 2097152 | tf_op jit(solution)/shard_map/all_to_all | solution.py:77
  76.3 32.1 %slice-start = ((s8[14680064]{0:T(1024)(128)(4,1)}), s8[4194304]{0:T(1024)(128)(4,1)S(1)}, s32[]{:S(2)}) async-start(s8[14680064]{0:T(1024)(128)(4,1)} %bitcast.40), calls=%async_computation.3 | async-start | bytes 8388608
  76.3 32.1 %slice-start.1 = ((s8[14680064]{0:T(1024)(128)(4,1)}), s8[4194304]{0:T(1024)(128)(4,1)S(1)}, s32[]{:S(2)}) async-start(s8[14680064]{0:T(1024)(128)(4,1)} %bitcast.40), calls=%async_computation.4 | async-start | bytes 8388608
  76.3 32.1 %slice-start.2 = ((s8[14680064]{0:T(1024)(128)(4,1)}), s8[4194304]{0:T(1024)(128)(4,1)S(1)}, s32[]{:S(2)}) async-start(s8[14680064]{0:T(1024)(128)(4,1)} %bitcast.40), calls=%async_computation.5 | async-start | bytes 8388608
  76.3 32.1 %slice-start.3 = ((s8[14680064]{0:T(1024)(128)(4,1)}), s8[2097152]{0:T(1024)(128)(4,1)S(1)}, s32[]{:S(2)}) async-start(s8[14680064]{0:T(1024)(128)(4,1)} %bitcast.40), calls=%async_computation.6 | async-start | bytes 4194304
  156.0 88.3 %all-to-all-start.1 = ((bf16[16,2,128]{2,1,0:T(2,128)(2,1)}), bf16[16,2,128]{2,1,0:T(2,128)(2,1)S(1)}, u32[]{:S(2)}, u32[]{:S(2)}) async-start(bf16[16,2,128]{2,1,0:T(2,128)(2,1)} %reshape.76), calls=%async_computation.1 | async-start | bytes 16384 | tf_op jit(solution)/shard_map/all_to_all | solution.py:81
  266.8 22.7 %copy-start.2 = (bf16[16,64,1792]{2,1,0:T(8,128)(2,1)S(1)}, bf16[16,64,1792]{2,1,0:T(8,128)(2,1)}, u32[]{:S(2)}) copy-start(bf16[16,64,1792]{2,1,0:T(8,128)(2,1)} %param.13) | copy-start | bytes 11010052
  266.8 27.4 %copy-start.1 = (bf16[1,8192,64]{1,2,0:T(8,128)(2,1)S(1)}, bf16[1,8192,64]{1,2,0:T(8,128)(2,1)}, u32[]{:S(2)}) copy-start(bf16[1,8192,64]{1,2,0:T(8,128)(2,1)} %param.12) | copy-start | bytes 3145732
Sparse Core Ops, SparseCore 0:
  9.5 96.8 all-gather.1
where the time goes:
time: 303 us; the launch traced here: 301 us
  local copies, waits for them, and re-layouts  145 us (48%)
  other arithmetic  77.6 us (26%)
  matrix products  28.8 us (10%)
  blocking collectives  22 us (7%)
  between operations  13.6 us (4%)
  starting transfers between devices  13.1 us (4%)
    another operation x3, other arithmetic, expand_sparse(): return jnp.stack(placed, axis=1).reshape(quarter * 4, width)  75.6 us
    reshape x1, local copies, waits for them, and re-layouts, expand_sparse(): return jnp.stack(placed, axis=1).reshape(quarter * 4, width)  45.2 us
    another operation x1, local copies, waits for them, and re-layouts, expand_sparse(): return jnp.stack(placed, axis=1).reshape(quarter * 4, width)  37.4 us
    reshape x1, local copies, waits for them, and re-layouts, expand_sparse(): pairs = values.reshape(quarter, 2, width)  29 us
    slice x1, local copies, waits for them, and re-layouts, expand_sparse(): value_two = pairs[:, 1, :]  28.5 us
    dot_general x1, matrix products, body(): jnp.dot(lax.all_gather(tokens, 'adapter', axis=0, tiled=True), dense, pre...  22.7 us
    all_gather x1, blocking collectives, body(): low_rows = lax.all_gather(own_low, 'adapter', axis=0, tiled=True)  22 us
    all_to_all x1, starting transfers between devices, body(): lax.all_to_all(outgoing, 'adapter', split_axis=0, concat_axis=0, tiled=True)  7.35 us
  transfers between devices with their start and end apart: 3, of which 0 were waited for; matrix products, arithmetic and copies ran while one was open for 74% of the time, Pallas kernels for 0%

commit v1 on v0

v1 whole, which is shorter than its diff:
```python
import functools

import jax
import jax.numpy as jnp
from jax import lax
from jax.experimental import pallas as pl
from jax.experimental.pallas import tpu as pltpu
from jax.sharding import PartitionSpec as P

ADAPTER_SCALE = 2.0
WAVES = 4
GROUPS = 128
MESH = pl.DeviceIdType.MESH
LEFT, RIGHT, ACROSS, TWIN = range(4)


def kernel(
    holders, across, capacity, slot_ref, tokens_ref, request_ref, values_hbm, pattern_hbm, down_hbm, up_hbm,
    out_ref, x, dense, total, vbuf, pbuf, down, down_p, up, low, low_all, spread, key,
    send_sem, recv_sem, low_send, low_recv, vsem, psem, misc_sem,
):
    rows_dev, width = tokens_ref.shape
    rows = rows_dev * holders
    hidden = up.shape[1]
    per_holder = holders * capacity
    line = holders // (2 * across)
    depth = 4 * GROUPS
    steps = width // depth
    wave_width = width // WAVES
    per_wave = wave_width // depth
    ticks = WAVES * line
    ratio = ticks // steps
    tn = 256 if hidden % 256 == 0 else 128
    me = lax.axis_index("adapter")
    core = lax.rem(me, 2)
    ypos = lax.rem(lax.div(me, 2), across)
    zpos = lax.div(me, 2 * across)

    def holder(z, y, c):
        return (z * across + y) * 2 + c

    def fetch(step):
        slot = lax.rem(step, 2)
        return (
            pltpu.make_async_copy(
                values_hbm.at[pl.ds(pl.multiple_of(step * 2 * GROUPS, 2 * GROUPS), 2 * GROUPS)],
                vbuf.at[slot], vsem.at[slot]),
            pltpu.make_async_copy(
                pattern_hbm.at[pl.ds(pl.multiple_of(step * GROUPS, GROUPS), GROUPS)],
                pbuf.at[slot], psem.at[slot]),
        )

    down_copy = pltpu.make_async_copy(down_hbm, down, misc_sem.at[0])
    up_copy = pltpu.make_async_copy(up_hbm, up, misc_sem.at[1])

    barrier = pltpu.get_barrier_semaphore()

    @pl.loop(1, holders)
    def _(i):
        pl.semaphore_signal(
            barrier, inc=1, device_id={"adapter": lax.rem(me + i, holders)}, device_id_type=MESH)

    for c in fetch(0):
        c.start()
    down_copy.start()
    up_copy.start()

    a = lax.broadcasted_iota(jnp.int32, (depth, depth), 0)
    b = lax.broadcasted_iota(jnp.int32, (depth, depth), 1)
    order = (a == 4 * (b & (GROUPS - 1)) + b // GROUPS).astype(jnp.float32).astype(jnp.bfloat16)
    order_t = (b == 4 * (a & (GROUPS - 1)) + a // GROUPS).astype(jnp.float32).astype(jnp.bfloat16)
    own_rows = pl.ds(pl.multiple_of(me * rows_dev, rows_dev), rows_dev)
    for s in range(steps):
        piece = jnp.dot(
            tokens_ref[:, s * depth:(s + 1) * depth], order, preferred_element_type=jnp.float32)
        x[s // per_wave, own_rows, (s % per_wave) * depth:(s % per_wave + 1) * depth] = piece.astype(
            jnp.bfloat16)

    pl.semaphore_wait(barrier, holders - 1)

    def copy(wave, owner, way):
        target = (
            holder(zpos - 1, ypos, core), holder(zpos + 1, ypos, core),
            holder(zpos, across - 1 - ypos, core), holder(zpos, ypos, 1 - core))[way]
        target = lax.rem(target + holders, holders)
        chunk = x.at[wave, pl.ds(pl.multiple_of(owner * rows_dev, rows_dev), rows_dev)]
        return pltpu.make_async_remote_copy(
            src_ref=chunk, dst_ref=chunk, send_sem=send_sem.at[wave, owner, way],
            recv_sem=recv_sem.at[wave, owner], device_id={"adapter": target}, device_id_type=MESH)

    def arrived(wave, owner):
        copy(wave, owner, TWIN).wait_recv()

    def ways_of_own(wave, do):
        @pl.when(zpos > 0)
        def _():
            do(copy(wave, me, LEFT))

        @pl.when(zpos < line - 1)
        def _():
            do(copy(wave, me, RIGHT))

        if across > 1:
            do(copy(wave, me, ACROSS))
        do(copy(wave, me, TWIN))

    def forwards(wave, hop, do, wait):
        @pl.when((hop < line - 1) & (zpos - 1 - hop >= 0))
        def _():
            owner = holder(zpos - 1 - hop, ypos, core)
            if wait:
                arrived(wave, owner)

            @pl.when(zpos < line - 1)
            def _():
                do(copy(wave, owner, RIGHT))

            if across > 1:
                do(copy(wave, owner, ACROSS))
            do(copy(wave, owner, TWIN))

        @pl.when((hop < line - 1) & (zpos + 1 + hop <= line - 1))
        def _():
            owner = holder(zpos + 1 + hop, ypos, core)
            if wait:
                arrived(wave, owner)

            @pl.when(zpos > 0)
            def _():
                do(copy(wave, owner, LEFT))

            if across > 1:
                do(copy(wave, owner, ACROSS))
            do(copy(wave, owner, TWIN))

    def from_across(wave, level, do, wait):
        if across == 1:
            return

        @pl.when(zpos - level >= 0)
        def _():
            owner = holder(zpos - level, across - 1 - ypos, core)
            if wait:
                arrived(wave, owner)
            do(copy(wave, owner, TWIN))

        @pl.when((level > 0) & (zpos + level <= line - 1))
        def _():
            owner = holder(zpos + level, across - 1 - ypos, core)
            if wait:
                arrived(wave, owner)
            do(copy(wave, owner, TWIN))

    start = lambda c: c.start()
    sent = lambda c: c.wait_send()

    ways_of_own(0, start)

    request = request_ref[...]
    slot = jnp.zeros(request.shape, jnp.int32)
    for i in range(holders):
        slot = jnp.where(request == i, slot_ref[i], slot)
    slot_f = slot.astype(jnp.float32)
    wide = jnp.broadcast_to(slot_f, (rows, 128))
    slot_row = jnp.transpose(wide)[0:1, :]
    ra = lax.broadcasted_iota(jnp.int32, (rows, rows), 0)
    rb = lax.broadcasted_iota(jnp.int32, (rows, rows), 1)
    before = (slot_f == slot_row) & (ra // rows_dev == rb // rows_dev) & (rb < ra)
    place = jnp.sum(before.astype(jnp.float32), axis=1, keepdims=True)
    block = (lax.broadcasted_iota(jnp.int32, (rows, 1), 0) // rows_dev).astype(jnp.float32)
    key[...] = jnp.broadcast_to(slot_f * per_holder + block * capacity + place, (rows, 128))

    total[...] = jnp.zeros_like(total)
    low[...] = jnp.zeros_like(low)
    down_copy.wait()

    qa = lax.broadcasted_iota(jnp.int32, (2 * GROUPS, 2 * GROUPS), 0)
    qb = lax.broadcasted_iota(jnp.int32, (2 * GROUPS, 2 * GROUPS), 1)
    pairs = (qb == 2 * (8 * (qa // 16) + (qa & 7)) + ((qa // 8) & 1)).astype(jnp.float32).astype(
        jnp.bfloat16)

    def expand(step):
        @pl.when(step + 1 < steps)
        def _():
            for c in fetch(step + 1):
                c.start()

        for c in fetch(step):
            c.wait()
        slot = lax.rem(step, 2)
        base = step * depth
        for j in range(hidden // tn):
            cols = pl.ds(j * tn, tn)
            both = jnp.dot(pairs, vbuf[slot, :, cols], preferred_element_type=jnp.float32)
            both = both.reshape(GROUPS // 8, 2, 8, tn)
            one = both[:, 0].reshape(GROUPS, tn)
            two = both[:, 1].reshape(GROUPS, tn)
            p = pbuf[slot, :, cols]
            zero = jnp.zeros_like(one)
            planes = (
                jnp.where(p < 3, one, zero),
                jnp.where(p == 0, two, jnp.where((p == 3) | (p == 4), one, zero)),
                jnp.where(p == 5, one, jnp.where((p == 1) | (p == 3), two, zero)),
                jnp.where((p == 2) | (p >= 4), two, zero),
            )
            for k, plane in enumerate(planes):
                dense[pl.ds(pl.multiple_of(base + k * GROUPS, GROUPS), GROUPS), cols] = plane.astype(
                    jnp.bfloat16)
        here = pl.ds(pl.multiple_of(base, depth), depth)
        part = jnp.dot(order_t, down[here, :], preferred_element_type=jnp.float32).astype(jnp.bfloat16)
        down_p[here, :] = jnp.concatenate([part, part], axis=1)

    def all_here(wave):
        @pl.loop(0, holders // 2)
        def _(i):
            arrived(wave, 2 * i + 1 - core)

    def low_of(wave):
        here = pl.ds(pl.multiple_of(wave * wave_width, wave_width), wave_width)
        low[...] += jnp.dot(x[wave], down_p[here, :], preferred_element_type=jnp.float32)

    def multiply(wave):
        here = pl.ds(pl.multiple_of(wave * wave_width, wave_width), wave_width)

        @pl.loop(0, hidden // tn)
        def _(j):
            cols = pl.ds(pl.multiple_of(j * tn, tn), tn)
            total[:, cols] += jnp.dot(
                x[wave], dense[here, cols], preferred_element_type=jnp.float32)

    @pl.loop(0, ticks)
    def _(t):
        wave, hop = lax.div(t, line), lax.rem(t, line)

        @pl.when(lax.rem(t, ratio) == 0)
        def _():
            expand(lax.div(t, ratio))

        @pl.when((hop == 0) & (wave + 1 < WAVES))
        def _():
            ways_of_own(wave + 1, start)

        forwards(wave, hop, start, True)

        @pl.when(t > 0)
        def _():
            from_across(lax.div(t - 1, line), lax.rem(t - 1, line), start, True)

        @pl.when((hop == 1) & (wave > 0))
        def _():
            all_here(wave - 1)
            low_of(wave - 1)
            multiply(wave - 1)

    from_across(WAVES - 1, line - 1, start, True)
    all_here(WAVES - 1)
    low_of(WAVES - 1)

    key_row = jnp.transpose(key[...])[0:1, :]
    mine = lax.broadcasted_iota(jnp.int32, (per_holder, rows), 0) + me * per_holder
    pick = (mine.astype(jnp.float32) == key_row).astype(jnp.float32).astype(jnp.bfloat16)
    low_all[me] = jnp.dot(
        pick, low[...].astype(jnp.bfloat16), preferred_element_type=jnp.float32).astype(jnp.bfloat16)

    def low_copy(owner, target):
        return pltpu.make_async_remote_copy(
            src_ref=low_all.at[owner], dst_ref=low_all.at[owner], send_sem=low_send.at[target],
            recv_sem=low_recv.at[owner], device_id={"adapter": target}, device_id_type=MESH)

    @pl.loop(1, holders)
    def _(i):
        low_copy(me, lax.rem(me + i, holders)).start()

    multiply(WAVES - 1)
    up_copy.wait()

    @pl.loop(1, holders)
    def _(i):
        low_copy(lax.rem(me + i, holders), lax.rem(me + i, holders)).wait_recv()

    tall = low_all[...].reshape(holders * per_holder, 128)
    names = lax.broadcasted_iota(jnp.int32, (rows, holders * per_holder), 1).astype(jnp.float32)
    choose = (names == key[:, 0:1]).astype(jnp.float32).astype(jnp.bfloat16)
    rows_low = ADAPTER_SCALE * jnp.dot(choose, tall, preferred_element_type=jnp.float32)
    rank = up.shape[0] // holders
    first = key[...]
    lane = lax.broadcasted_iota(jnp.int32, (rows, 128), 1) // rank
    for j in range(up.shape[0] // 128):
        least = ((lane + (128 // rank) * j) * per_holder).astype(jnp.float32)
        held = (first >= least) & (first < least + per_holder)
        spread[:, j * 128:(j + 1) * 128] = jnp.where(held, rows_low, 0.0).astype(jnp.bfloat16)

    @pl.loop(0, hidden // tn)
    def _(j):
        cols = pl.ds(pl.multiple_of(j * tn, tn), tn)
        out_ref[:, cols] = (
            total[:, cols] + jnp.dot(spread[...], up[:, cols], preferred_element_type=jnp.float32)
        ).astype(jnp.bfloat16)

    @pl.loop(1, holders)
    def _(i):
        low_copy(me, lax.rem(me + i, holders)).wait_send()

    @pl.loop(0, WAVES)
    def _(wave):
        ways_of_own(wave, sent)

    @pl.loop(0, ticks)
    def _(t):
        wave, hop = lax.div(t, line), lax.rem(t, line)
        forwards(wave, hop, sent, False)
        from_across(wave, hop, sent, False)


def body(tokens, values, pattern, request, slots, down, up):
    holders = lax.axis_size("adapter")
    rows_dev, width = tokens.shape
    rows = rows_dev * holders
    adapters, rank, hidden = up.shape
    across = 2 if holders == 16 else 1
    capacity = max(2, 2 * rows_dev // holders)
    bf16, f32 = jnp.bfloat16, jnp.float32
    anywhere = pl.BlockSpec(memory_space=pl.ANY)
    vmem = pl.BlockSpec(memory_space=pltpu.VMEM)
    dma = pltpu.SemaphoreType.DMA
    return pl.pallas_call(
        functools.partial(kernel, holders, across, capacity),
        out_shape=jax.ShapeDtypeStruct((rows, hidden), bf16),
        in_specs=[pl.BlockSpec(memory_space=pltpu.SMEM), vmem, vmem] + [anywhere] * 4,
        out_specs=vmem,
        scratch_shapes=[
            pltpu.VMEM((WAVES, rows, width // WAVES), bf16),
            pltpu.VMEM((width, hidden), bf16),
            pltpu.VMEM((rows, hidden), f32),
            pltpu.VMEM((2, 2 * GROUPS, hidden), bf16),
            pltpu.VMEM((2, GROUPS, hidden), jnp.int32),
            pltpu.VMEM((width, rank), bf16),
            pltpu.VMEM((width, 2 * rank), bf16),
            pltpu.VMEM((adapters * rank, hidden), bf16),
            pltpu.VMEM((rows, 2 * rank), f32),
            pltpu.VMEM((holders, holders * capacity, 2 * rank), bf16),
            pltpu.VMEM((rows, adapters * rank), bf16),
            pltpu.VMEM((rows, 128), f32),
            dma((WAVES, holders, 4)),
            dma((WAVES, holders)),
            dma((holders,)),
            dma((holders,)),
            dma((2,)),
            dma((2,)),
            dma((2,)),
        ],
        compiler_params=pltpu.CompilerParams(
            collective_id=0, has_side_effects=True, vmem_limit_bytes=62 * 1024 * 1024),
        cost_estimate=pl.CostEstimate(
            flops=2 * rows * width * hidden, bytes_accessed=40 * 1024 * 1024, transcendentals=0),
    )(slots, tokens, request, values, pattern, down.reshape(width, rank), up.reshape(adapters * rank, hidden))


def solution(mesh):
    placed = (
        P(("group", "adapter"), None),
        P(None, "adapter"),
        P(None, "adapter"),
        P("group", None),
        P(),
        P("adapter", None, None),
        P(None, None, "adapter"),
    )
    return jax.shard_map(
        body, mesh=mesh, in_specs=placed, out_specs=P("group", "adapter"), check_vma=False
    )
```

time: 303 us -> 95.9 us (0.32)
  local copies, waits for them, and re-layouts: 145 us -> 7.16 us
  Pallas kernels: 0 us -> 88.3 us
  other arithmetic: 77.6 us -> 0 us
  matrix products: 28.8 us -> 0 us
  blocking collectives: 22 us -> 0 us
  between operations: 13.6 us -> 0.01 us
  starting transfers between devices: 13.1 us -> 0 us
    pallas_call x0 -> x1, Pallas kernels: none -> 88.3 us  [body(): pl.pallas_call(functools.partial(kernel, holders, across, capacity), out_...]
    another operation x3 -> x0, other arithmetic: 75.6 us -> none  [expand_sparse(): return jnp.stack(placed, axis=1).reshape(quarter * 4, width)]
    reshape x5 -> x0, local copies, waits for them, and re-layouts: 75.6 us -> none  [the longest x1 45.2 us: expand_sparse(): return jnp.stack(placed, axis=1).reshape(quarter * 4, width)]
    another operation x1 -> x0, local copies, waits for them, and re-layouts: 37.4 us -> none  [expand_sparse(): return jnp.stack(placed, axis=1).reshape(quarter * 4, width)]
    dot_general x5 -> x0, matrix products: 28.8 us -> none  [the longest x1 22.7 us: body(): jnp.dot(lax.all_gather(tokens, 'adapter', axis=0, tiled=True), dense, pre...]
    slice x1 -> x0, local copies, waits for them, and re-layouts: 28.5 us -> none  [expand_sparse(): value_two = pairs[:, 1, :]]
    all_gather x1 -> x0, blocking collectives: 22 us -> none  [body(): low_rows = lax.all_gather(own_low, 'adapter', axis=0, tiled=True)]
    all_to_all x2 -> x0, starting transfers between devices: 13.1 us -> none  [the longest x1 7.35 us: body(): lax.all_to_all(outgoing, 'adapter', split_axis=0, concat_axis=0, tiled=True)]
  transfers between devices with their start and end apart: 3 -> 0, of which waited for: 0 -> 0; matrix products, arithmetic and copies ran while one was open for 74% -> 0% of each run, Pallas kernels for 0% -> 0%
where the time goes in v1:
time: 95.9 us; the launch traced here: 95.5 us
  Pallas kernels  88.3 us (92%)
  local copies, waits for them, and re-layouts  7.16 us (7%)
    pallas_call x1, Pallas kernels, body(): pl.pallas_call(functools.partial(kernel, holders, across, capacity), out_...  88.3 us
    unnamed x3, local copies, waits for them, and re-layouts  7.16 us

profile of v1, /device:TPU:1, one launch (start us, length us, event | category | flops | bytes accessed | tf_op | source)
XLA Modules:
  0.0 95.5 jit_solution(4213784873164409684)
XLA Ops:
  0.0 1.5 %copy.9.request_ref = s32[512,1]{1,0:T(8,128)} copy(s32[512,1]{0,1:T(1,128)} %param.10) | data formatting | bytes 4096 | tf_op args[3]
  1.5 2.8 %copy.8 = bf16[1,8192,64]{2,1,0:T(8,128)(2,1)} copy(bf16[1,8192,64]{1,2,0:T(8,128)(2,1)} %param.12) | data formatting | bytes 2097152 | tf_op args[5]
  4.3 88.3 %shard_map.73 = bf16[512,1792]{1,0:T(8,128)(2,1)} custom-call(s32[16]{0:T(128)} %slot_ref.1, bf16[32,8192]{1,0:T(8,128)(2,1)} %tokens_ref.1, s32[512,1]{1,0:T(8,128)} %copy.9.request_ref, bf16[4096,1792]{1,0:T(8,128)(2,1)} %values_hbm.1, s32[2048,1792]{1,0:T(8,128)} %pattern_hbm.1, bf16[8192,64]{1,0:T(8,128)(2,1)} %bitcast.2, bf16[1024,1792]{1,0:T(8,128)(2,1)} %bitcast.3), custom_call_target="tpu_custom_call" | custom-call | flops 15032385536 | bytes 41943040 | tf_op jit(solution)/shard_map/pallas_call | solution.py:326
  92.6 2.8 %copy.11 = bf16[512,1792]{1,0:T(8,128)(2,1)} copy(bf16[512,1792]{1,0:T(8,128)(2,1)} %shard_map.73) | data formatting | bytes 3670016

commit v2 on v1

--- a/solution.py
+++ b/solution.py
@@ -8,7 +8,8 @@
 from jax.sharding import PartitionSpec as P
 
 ADAPTER_SCALE = 2.0
-WAVES = 4
+WAVES = 2
+CHUNK = 256
 GROUPS = 128
 MESH = pl.DeviceIdType.MESH
 LEFT, RIGHT, ACROSS, TWIN = range(4)
@@ -29,7 +30,8 @@
     wave_width = width // WAVES
     per_wave = wave_width // depth
     ticks = WAVES * line
-    ratio = ticks // steps
+    ratio = max(1, ticks // steps)
+    per_tick = max(1, steps // ticks)
     tn = 256 if hidden % 256 == 0 else 128
     me = lax.axis_index("adapter")
     core = lax.rem(me, 2)
@@ -65,16 +67,24 @@
     down_copy.start()
     up_copy.start()
 
-    a = lax.broadcasted_iota(jnp.int32, (depth, depth), 0)
-    b = lax.broadcasted_iota(jnp.int32, (depth, depth), 1)
-    order = (a == 4 * (b & (GROUPS - 1)) + b // GROUPS).astype(jnp.float32).astype(jnp.bfloat16)
-    order_t = (b == 4 * (a & (GROUPS - 1)) + a // GROUPS).astype(jnp.float32).astype(jnp.bfloat16)
+    a = lax.broadcasted_iota(jnp.int32, (CHUNK, CHUNK), 0)
+    b = lax.broadcasted_iota(jnp.int32, (CHUNK, CHUNK), 1)
+    order = (a == 4 * (b & (CHUNK // 4 - 1)) + b // (CHUNK // 4)).astype(jnp.float32).astype(jnp.bfloat16)
     own_rows = pl.ds(pl.multiple_of(me * rows_dev, rows_dev), rows_dev)
-    for s in range(steps):
-        piece = jnp.dot(
-            tokens_ref[:, s * depth:(s + 1) * depth], order, preferred_element_type=jnp.float32)
-        x[s // per_wave, own_rows, (s % per_wave) * depth:(s % per_wave + 1) * depth] = piece.astype(
-            jnp.bfloat16)
+    chunks = wave_width // CHUNK
+
+    def reorder(source, wave):
+        high = source.shape[0]
+        pieces = [source[:, (wave * chunks + i) * CHUNK:(wave * chunks + i + 1) * CHUNK] for i in range(chunks)]
+        moved = jnp.dot(
+            jnp.concatenate(pieces, axis=0), order, preferred_element_type=jnp.float32).astype(jnp.bfloat16)
+        return [moved[i * high:(i + 1) * high] for i in range(chunks)]
+
+    def reorder_tokens(wave):
+        for i, piece in enumerate(reorder(tokens_ref, wave)):
+            x[wave, own_rows, i * CHUNK:(i + 1) * CHUNK] = piece
+
+    reorder_tokens(0)
 
     pl.semaphore_wait(barrier, holders - 1)
 
@@ -155,14 +165,15 @@
     sent = lambda c: c.wait_send()
 
     ways_of_own(0, start)
+    for wave in range(1, WAVES):
+        reorder_tokens(wave)
 
     request = request_ref[...]
     slot = jnp.zeros(request.shape, jnp.int32)
     for i in range(holders):
         slot = jnp.where(request == i, slot_ref[i], slot)
-    slot_f = slot.astype(jnp.float32)
-    wide = jnp.broadcast_to(slot_f, (rows, 128))
-    slot_row = jnp.transpose(wide)[0:1, :]
+    slot_row = slot.astype(jnp.float32)
+    slot_f = jnp.transpose(jnp.broadcast_to(slot_row, (128, rows)))[:, 0:1]
     ra = lax.broadcasted_iota(jnp.int32, (rows, rows), 0)
     rb = lax.broadcasted_iota(jnp.int32, (rows, rows), 1)
     before = (slot_f == slot_row) & (ra // rows_dev == rb // rows_dev) & (rb < ra)
@@ -173,6 +184,9 @@
     total[...] = jnp.zeros_like(total)
     low[...] = jnp.zeros_like(low)
     down_copy.wait()
+    for wave in range(WAVES):
+        for i, piece in enumerate(reorder(down, wave)):
+            down_p[wave, :, i * CHUNK:(i + 1) * CHUNK] = jnp.concatenate([piece, piece], axis=0)
 
     qa = lax.broadcasted_iota(jnp.int32, (2 * GROUPS, 2 * GROUPS), 0)
     qb = lax.broadcasted_iota(jnp.int32, (2 * GROUPS, 2 * GROUPS), 1)
@@ -193,9 +207,9 @@
             cols = pl.ds(j * tn, tn)
             both = jnp.dot(pairs, vbuf[slot, :, cols], preferred_element_type=jnp.float32)
             both = both.reshape(GROUPS // 8, 2, 8, tn)
-            one = both[:, 0].reshape(GROUPS, tn)
-            two = both[:, 1].reshape(GROUPS, tn)
-            p = pbuf[slot, :, cols]
+            one = both[:, 0].reshape(GROUPS, tn).astype(jnp.bfloat16)
+            two = both[:, 1].reshape(GROUPS, tn).astype(jnp.bfloat16)
+            p = pbuf[slot, :, cols].astype(jnp.float32).astype(jnp.bfloat16)
             zero = jnp.zeros_like(one)
             planes = (
                 jnp.where(p < 3, one, zero),
@@ -203,12 +217,11 @@
                 jnp.where(p == 5, one, jnp.where((p == 1) | (p == 3), two, zero)),
                 jnp.where((p == 2) | (p >= 4), two, zero),
             )
+            quarter = CHUNK // 4
             for k, plane in enumerate(planes):
-                dense[pl.ds(pl.multiple_of(base + k * GROUPS, GROUPS), GROUPS), cols] = plane.astype(
-                    jnp.bfloat16)
-        here = pl.ds(pl.multiple_of(base, depth), depth)
-        part = jnp.dot(order_t, down[here, :], preferred_element_type=jnp.float32).astype(jnp.bfloat16)
-        down_p[here, :] = jnp.concatenate([part, part], axis=1)
+                for u in range(GROUPS // quarter):
+                    place = pl.multiple_of(base + u * CHUNK + k * quarter, quarter)
+                    dense[pl.ds(place, quarter), cols] = plane[u * quarter:(u + 1) * quarter]
 
     def all_here(wave):
         @pl.loop(0, holders // 2)
@@ -216,13 +229,13 @@
             arrived(wave, 2 * i + 1 - core)
 
     def low_of(wave):
+        low[...] += lax.dot_general(
+            x[wave], down_p[wave], (((1,), (1,)), ((), ())), preferred_element_type=jnp.float32)
+
+    def multiply(wave, least, most):
         here = pl.ds(pl.multiple_of(wave * wave_width, wave_width), wave_width)
-        low[...] += jnp.dot(x[wave], down_p[here, :], preferred_element_type=jnp.float32)
-
-    def multiply(wave):
-        here = pl.ds(pl.multiple_of(wave * wave_width, wave_width), wave_width)
-
-        @pl.loop(0, hidden // tn)
+
+        @pl.loop(least, most)
         def _(j):
             cols = pl.ds(pl.multiple_of(j * tn, tn), tn)
             total[:, cols] += jnp.dot(
@@ -234,7 +247,9 @@
 
         @pl.when(lax.rem(t, ratio) == 0)
         def _():
-            expand(lax.div(t, ratio))
+            @pl.loop(0, per_tick)
+            def _(i):
+                expand(lax.div(t, ratio) * per_tick + i)
 
         @pl.when((hop == 0) & (wave + 1 < WAVES))
         def _():
@@ -250,7 +265,11 @@
         def _():
             all_here(wave - 1)
             low_of(wave - 1)
-            multiply(wave - 1)
+
+        @pl.when((hop > 0) & (wave > 0))
+        def _():
+            tiles = hidden // tn
+            multiply(wave - 1, lax.div(tiles * (hop - 1), line - 1), lax.div(tiles * hop, line - 1))
 
     from_across(WAVES - 1, line - 1, start, True)
     all_here(WAVES - 1)
@@ -271,7 +290,7 @@
     def _(i):
         low_copy(me, lax.rem(me + i, holders)).start()
 
-    multiply(WAVES - 1)
+    multiply(WAVES - 1, 0, hidden // tn)
     up_copy.wait()
 
     @pl.loop(1, holders)
@@ -334,8 +353,8 @@
             pltpu.VMEM((rows, hidden), f32),
             pltpu.VMEM((2, 2 * GROUPS, hidden), bf16),
             pltpu.VMEM((2, GROUPS, hidden), jnp.int32),
-            pltpu.VMEM((width, rank), bf16),
-            pltpu.VMEM((width, 2 * rank), bf16),
+            pltpu.VMEM((rank, width), bf16),
+            pltpu.VMEM((WAVES, 2 * rank, width // WAVES), bf16),
             pltpu.VMEM((adapters * rank, hidden), bf16),
             pltpu.VMEM((rows, 2 * rank), f32),
             pltpu.VMEM((holders, holders * capacity, 2 * rank), bf16),
@@ -353,7 +372,7 @@
             collective_id=0, has_side_effects=True, vmem_limit_bytes=62 * 1024 * 1024),
         cost_estimate=pl.CostEstimate(
             flops=2 * rows * width * hidden, bytes_accessed=40 * 1024 * 1024, transcendentals=0),
-    )(slots, tokens, request, values, pattern, down.reshape(width, rank), up.reshape(adapters * rank, hidden))
+    )(slots, tokens, request.reshape(1, rows), values, pattern, down[0].T, up.reshape(adapters * rank, hidden))
 
 
 def solution(mesh):

time: 95.9 us -> 82.8 us (0.86)
  Pallas kernels: 88.3 us -> 79.7 us
  local copies, waits for them, and re-layouts: 7.16 us -> 2.85 us
    pallas_call x1, Pallas kernels: 88.3 us -> 79.7 us  [body(): pl.pallas_call(functools.partial(kernel, holders, across, capacity), out_...]
    unnamed x3 -> x1, local copies, waits for them, and re-layouts: 7.16 us -> 2.85 us
where the time goes in v2:
time: 82.8 us; the launch traced here: 82.5 us
  Pallas kernels  79.7 us (96%)
  local copies, waits for them, and re-layouts  2.85 us (3%)
    pallas_call x1, Pallas kernels, body(): pl.pallas_call(functools.partial(kernel, holders, across, capacity), out_...  79.7 us
    unnamed x1, local copies, waits for them, and re-layouts  2.85 us

profile of v2, /device:TPU:1, one launch (start us, length us, event | category | flops | bytes accessed | tf_op | source)
XLA Modules:
  0.0 82.5 jit_solution(8953056616136571666)
XLA Ops:
  0.0 79.7 %shard_map.73 = bf16[512,1792]{1,0:T(8,128)(2,1)} custom-call(s32[16]{0:T(128)} %slot_ref.1, bf16[32,8192]{1,0:T(8,128)(2,1)} %tokens_ref.1, s32[1,512]{1,0:T(1,128)} %bitcast.7, bf16[4096,1792]{1,0:T(8,128)(2,1)} %values_hbm.1, s32[2048,1792]{1,0:T(8,128)} %pattern_hbm.1, bf16[64,8192]{1,0:T(8,128)(2,1)} %bitcast.6, bf16[1024,1792]{1,0:T(8,128)(2,1)} %bitcast.5), custom_call_target="tpu_custom_call" | custom-call | flops 15032385536 | bytes 41943040 | tf_op jit(solution)/shard_map/pallas_call | solution.py:345
  79.7 2.8 %copy.9 = bf16[512,1792]{1,0:T(8,128)(2,1)} copy(bf16[512,1792]{1,0:T(8,128)(2,1)} %shard_map.73) | data formatting | bytes 3670016
